TPU v7x, 256 devices: a whole 4x4x8 slice. The times are simulated.
256 devices in a mesh: row: 8 (over z), col: 32 (over y, x, core).
Axes of the slice: x: 4, y: 4, z: 8, core: 2. Of those that a mesh axis runs over, the one named last changes fastest.
Arguments:
- matrix: bfloat16 [6, 4096, 2, 16384], P(None, 'row', None, 'col'), may hold values from -6 to 6
- lower_inv: bfloat16 [2, 512, 512], replicated, as said below
- upper_inv: bfloat16 [2, 512, 512], replicated, as said below
Outputs:
- factored: bfloat16 [6, 4096, 2, 16384], P(None, 'row', None, 'col')
Inputs may be any that keep to these rules, and one draw needn't show every extreme that they name: Each lower_inv[k] is unit lower triangular. Each upper_inv[k] is upper triangular with a positive diagonal.
All inputs are finite; a program needn't handle non-finite values.
Results may differ from a plain program's by a relative error of at most 0.0076.
Values may be sent and summed in bfloat16 or wider, within the bound.
A program may use at most 128 MiB of HBM per device.

v0:
```python
import jax
import jax.numpy as jnp
from jax import lax
from jax.sharding import PartitionSpec as P


def broadcast(block, axis, source):
    block = jnp.where(lax.axis_index(axis) == source, block, jnp.zeros_like(block))
    return lax.psum(block, axis)


def tile_ids(count, tile_size, stride, index):
    ids = jnp.arange(count, dtype=jnp.int32) * stride + index
    return jnp.broadcast_to(ids[:, None], (count, tile_size)).reshape(count * tile_size)


def solve_lower(owner, block, upper_k):

    def compute(blk):
        return jnp.dot(
            blk.astype(jnp.bfloat16), upper_k, preferred_element_type=jnp.float32
        ).astype(jnp.bfloat16)

    def nothing(blk):
        return jnp.zeros((blk.shape[0], upper_k.shape[1]), jnp.bfloat16)

    return lax.cond(owner, compute, nothing, block)


def solve_upper(owner, block, lower_k):

    def compute(blk):
        return jnp.dot(
            lower_k, blk.astype(jnp.bfloat16), preferred_element_type=jnp.float32
        ).astype(jnp.bfloat16)

    def nothing(blk):
        return jnp.zeros((lower_k.shape[0], blk.shape[1]), jnp.bfloat16)

    return lax.cond(owner, compute, nothing, block)


def panels(col_block, row_block, lower_k, upper_k, col_owner, row_owner, step):
    lower = broadcast(solve_lower(col_owner, col_block, upper_k), "col", step)
    upper = broadcast(solve_upper(row_owner, row_block, lower_k), "row", step)
    return (lower, upper)


def keep_rows(panel, flags):
    return jnp.where(flags[:, None], panel, jnp.zeros_like(panel))


def keep_cols(panel, flags):
    return jnp.where(flags[None, :], panel, jnp.zeros_like(panel))


def write_column(schur, lower, flags, tile_size):
    block = jnp.where(flags[:, None], lower.astype(jnp.float32), schur[:, :tile_size])
    return schur.at[:, :tile_size].set(block)


def write_row(schur, upper, flags, tile_size):
    block = jnp.where(flags[None, :], upper.astype(jnp.float32), schur[:tile_size, :])
    return schur.at[:tile_size, :].set(block)


def on_device(matrix, lower_inv, upper_inv):
    row_tiles, tile_size, col_tiles, _ = matrix.shape
    row_index = lax.axis_index("row")
    col_index = lax.axis_index("col")
    row_ids = tile_ids(row_tiles, tile_size, lax.axis_size("row"), row_index)
    col_ids = tile_ids(col_tiles, tile_size, lax.axis_size("col"), col_index)
    initial = matrix.reshape(row_tiles * tile_size, col_tiles * tile_size)
    lower_first, upper_first = panels(
        initial[:, :tile_size],
        initial[:tile_size, :],
        lower_inv[0],
        upper_inv[0],
        col_index == 0,
        row_index == 0,
        0,
    )
    left_first = keep_rows(lower_first, row_ids > 0)
    right_first = keep_cols(upper_first, col_ids > 0)
    schur = initial.astype(jnp.float32) - jnp.dot(
        left_first, right_first, preferred_element_type=jnp.float32
    )
    lower_second, upper_second = panels(
        schur[:, :tile_size],
        schur[:tile_size, :],
        lower_inv[1],
        upper_inv[1],
        col_index == 1,
        row_index == 1,
        1,
    )
    left_second = keep_rows(lower_second, row_ids > 1)
    right_second = keep_cols(upper_second, col_ids > 1)
    schur = schur - jnp.dot(left_second, right_second, preferred_element_type=jnp.float32)
    schur = write_column(schur, lower_first, (row_ids > 0) & (col_index == 0), tile_size)
    schur = write_column(schur, lower_second, (row_ids > 1) & (col_index == 1), tile_size)
    schur = write_row(schur, upper_first, (col_ids > 0) & (row_index == 0), tile_size)
    schur = write_row(schur, upper_second, (col_ids > 1) & (row_index == 1), tile_size)
    return schur.astype(jnp.bfloat16).reshape(matrix.shape)


def solution(mesh):
    placed = (P(None, "row", None, "col"), P(), P())
    return jax.shard_map(
        on_device,
        mesh=mesh,
        in_specs=placed,
        out_specs=P(None, "row", None, "col"),
        check_vma=False,
    )
```

profile of v0, /device:TPU:77, one launch (start us, length us, event | category | flops | bytes accessed | tf_op | source)
XLA Modules:
  0.0 456.4 jit_solution(3093414542680500413)
XLA Ops:
  6.5 0.1 conditional.5
  6.5 0.1 broadcast.154
  6.7 1.0 broadcast_select_fusion.3
  7.8 7.5 %copy.5 = bf16[384,8,2,512]{3,1,2,0:T(8,128)(2,1)} copy(bf16[384,8,2,512]{3,2,1,0:T(2,128)(2,1)} %bitcast.19) | data formatting | bytes 12582912
  15.3 0.2 conditional.4
  15.3 0.2 broadcast.153
  15.6 1.8 broadcast_select_fusion.1
  17.5 0.1 broadcast_in_dim.76
  17.6 0.1 broadcast_in_dim.78
  17.7 64.9 %all-reduce.7.cloned.1.call-done = bf16[512,1024]{1,0:T(8,128)(2,1)} async-done(((bf16[512,1024]{1,0:T(8,128)(2,1)}), bf16[512,1024]{1,0:T(8,128)(2,1)}) %all-reduce.7.cloned.1.call-update) | async-done | bytes 1048592 | tf_op jit(solution)/shard_map/psum | solution.py:9
  82.6 124.1 %all-reduce.5.cloned.1.call-done = bf16[3072,512]{1,0:T(8,128)(2,1)} async-done(((bf16[3072,512]{1,0:T(8,128)(2,1)}), bf16[3072,512]{1,0:T(8,128)(2,1)}) %all-reduce.5.cloned.1.call-update) | async-done | bytes 3145744 | tf_op jit(solution)/shard_map/psum | solution.py:9
  206.6 9.7 %convert_subtract_fusion = f32[3072,1024]{1,0:T(8,128)} fusion(bf16[3072,1024]{1,0:T(8,128)(2,1)} %bitcast.21, bf16[3072,512]{1,0:T(8,128)(2,1)} %all-reduce.5.cloned.1.call-done, pred[3072]{0:T(1024)(128)(4,1)S(1)} %gt.61, bf16[512,1024]{1,0:T(8,128)(2,1)} %all-reduce.7.cloned.1.call-done, pred[1024]{0:T(1024)(128)(4,1)S(1)} %gt.63), kind=kOutput, calls=%fused_computation.15 | convolution fusion | flops 3229614080 | bytes 23072768 | tf_op jit(solution)/shard_map/dot_general | solution.py:85
  216.4 0.1 conditional.7
  216.4 0.1 broadcast.156
  216.5 1.0 broadcast_select_fusion.2
  217.6 0.4 conditional.6
  217.6 0.2 broadcast.155
  218.0 1.9 broadcast_select_fusion
  219.9 0.1 broadcast_in_dim.80
  220.0 0.1 broadcast_in_dim.82
  220.1 0.7 compare_reduce_fusion
  220.8 69.9 %all-reduce.11.cloned.1.call-done = bf16[512,1024]{1,0:T(8,128)(2,1)} async-done(((bf16[512,1024]{1,0:T(8,128)(2,1)}), bf16[512,1024]{1,0:T(8,128)(2,1)}) %all-reduce.11.cloned.1.call-update) | async-done | bytes 1048592 | tf_op jit(solution)/shard_map/psum | solution.py:9
  290.7 124.0 %all-reduce.9.cloned.1.call-done = bf16[3072,512]{1,0:T(8,128)(2,1)} async-done(((bf16[3072,512]{1,0:T(8,128)(2,1)}), bf16[3072,512]{1,0:T(8,128)(2,1)}) %all-reduce.9.cloned.1.call-update) | async-done | bytes 3145744 | tf_op jit(solution)/shard_map/psum | solution.py:9
  414.8 8.0 %convolution_subtract_fusion = bf16[3072,1024]{1,0:T(8,128)(2,1)S(1)} fusion(f32[3072,1024]{1,0:T(8,128)} %convert_subtract_fusion, bf16[3072,512]{1,0:T(8,128)(2,1)} %all-reduce.9.cloned.1.call-done, pred[3072]{0:T(1024)(128)(4,1)S(1)} %gt.65, bf16[512,1024]{1,0:T(8,128)(2,1)} %all-reduce.11.cloned.1.call-done, pred[1024]{0:T(1024)(128)(4,1)S(1)} %gt.67), kind=kOutput, calls=%fused_computation.19 | convolution fusion | flops 3229614080 | bytes 23072768 | tf_op jit(solution)/shard_map/dot_general | solution.py:99
  422.8 0.7 copy.18
  423.6 1.1 copy-done
  424.7 2.8 fusion.10
  427.6 4.2 fusion.9
  431.8 2.6 copy.20
  434.4 2.7 fusion.17
  437.1 1.6 select_dynamic-update-slice_fusion
  438.7 11.1 %reshape.160 = bf16[6,512,2,512]{3,2,1,0:T(2,128)(2,1)} reshape(bf16[3072,1024]{1,0:T(8,128)(2,1)} %select_dynamic-update-slice_fusion) | data formatting | bytes 12582912 | tf_op jit(solution)/shard_map/reshape | solution.py:104
  (27 shorter events, 0.3 us)
Async XLA Ops:
  6.5 76.0 %all-reduce.7.cloned.1.call-start = ((), (), s32[]{:S(2)}) async-start(), calls=%async_computation.1 | async-start | bytes 2097152 | tf_op jit(solution)/shard_map/psum | solution.py:9
  7.7 198.9 %all-reduce.5.cloned.1.call-start = ((), (), s32[]{:S(2)}) async-start(), calls=%async_computation | async-start | bytes 6291456 | tf_op jit(solution)/shard_map/psum | solution.py:9
  17.4 273.3 %all-reduce.11.cloned.1.call-start = ((), (), s32[]{:S(2)}) async-start(), calls=%async_computation.3 | async-start | bytes 2097152 | tf_op jit(solution)/shard_map/psum | solution.py:9
  17.7 198.7 %copy-start.4 = (bf16[2,512,512]{2,1,0:T(8,128)(2,1)S(1)}, bf16[2,512,512]{2,1,0:T(8,128)(2,1)}, u32[]{:S(2)}) copy-start(bf16[2,512,512]{2,1,0:T(8,128)(2,1)} %param.20) | copy-start | bytes 3145732
  217.6 197.2 %all-reduce.9.cloned.1.call-start = ((), (), s32[]{:S(2)}) async-start(), calls=%async_computation.2 | async-start | bytes 6291456 | tf_op jit(solution)/shard_map/psum | solution.py:9
  422.8 1.9 copy-start
  424.7 2.8 copy-start.2
  431.7 2.7 copy-start.1
  434.4 2.7 copy-start.3
Sparse Core Ops, SparseCore 0:
  9.7 72.8 all-reduce.6
  85.9 120.6 all-reduce.4
  217.7 73.0 all-reduce.10
  293.9 120.8 all-reduce.8
where the time goes:
time: 461 us; the launch traced here: 456 us
  waiting for transfers between devices  383 us (83%)
  local copies, waits for them, and re-layouts  24.2 us (5%)
  other arithmetic  17.8 us (4%)
  matrix products  17.7 us (4%)
  between operations  13.3 us (3%)
    psum x4, waiting for transfers between devices, broadcast(): return lax.psum(block, axis)  383 us
    unnamed x13, local copies, waits for them, and re-layouts  12.1 us
    reshape x1, local copies, waits for them, and re-layouts, on_device(): return schur.astype(jnp.bfloat16).reshape(matrix.shape)  11.1 us
    dot_general x1, matrix products, on_device(): jnp.dot(left_first, right_first, preferred_element_type=jnp.float32)  9.71 us
  transfers between devices with their start and end apart: 4, of which 4 were waited for; matrix products, arithmetic and copies ran while one was open for 3% of the time, Pallas kernels for 0%

commit v1 on v0

v1 whole, which is shorter than its diff:
```python
import functools

import jax
import jax.numpy as jnp
from jax import lax
from jax.experimental import pallas as pl
from jax.experimental.pallas import tpu as pltpu
from jax.sharding import PartitionSpec as P

MESH = pl.DeviceIdType.MESH
F32, BF16 = jnp.float32, jnp.bfloat16
NB = 512
SIDE = 4
STEPS = ((1, 0), (0, 1), (-1, 0), (0, -1))
ENTERED = {
    (1, 0): 0, (2, 0): 0, (3, 0): 0, (0, 1): 2, (1, 1): 1, (2, 1): 0, (3, 1): 0, (0, 2): 2,
    (1, 2): 1, (2, 2): 0, (3, 2): 0, (0, 3): 2, (1, 3): 3, (2, 3): 3, (3, 3): 0,
}
CHUNK = 64
ZCHUNK = 32
LAG, ZLAG = 5, 5


def trees():
    def depth_of(chip):
        depth = 0
        while chip != (0, 0):
            dx, dy = STEPS[ENTERED[chip]]
            chip, depth = ((chip[0] - dx) % SIDE, (chip[1] - dy) % SIDE), depth + 1
        return depth

    depth = [[0] * SIDE**2 for _ in range(4)]
    owner = [[4] * SIDE**2 for _ in range(4)]
    for t in range(4):
        for chip, step in ENTERED.items():
            x, y = chip
            for _ in range(t):
                x, y = -y % SIDE, x
            d = (step + t) % 4
            depth[t][y * SIDE + x] = depth_of(chip)
            parent = (y - STEPS[d][1]) % SIDE * SIDE + (x - STEPS[d][0]) % SIDE
            owner[d][parent] = t
    return depth, owner


DEPTH, OWNER = trees()
DEEPEST = max(max(row) for row in DEPTH)


def pick(table, index):
    value = jnp.int32(table[-1])
    for i in range(len(table) - 2, -1, -1):
        value = jnp.where(index == i, jnp.int32(table[i]), value)
    return value


def dot(a, b):
    return jnp.dot(a, b, preferred_element_type=F32)


def kernel(
    tiles, n_row, n_col, m_ref, lower_ref, upper_ref, out_ref, o_ref, wide, panel, rows, extra,
    load_sem, store_sem, panel_recv, panel_send, pair_recv, pair_send, row_recv, row_send,
):
    z, col = lax.axis_index("row"), lax.axis_index("col")
    core, chip = col % 2, col // 2
    x, y = chip % SIDE, chip // SIDE
    root = chip == 0
    plain = tiles * NB // (4 * CHUNK)
    more = NB // (4 * CHUNK)
    count = plain + more
    zcount = NB // ZCHUNK
    lines = 8 * NB

    peers = []
    for dx, dy in STEPS:
        peers.append({"col": ((y + dy) % SIDE * SIDE + (x + dx) % SIDE) * 2 + core})
    pair = {"col": chip * 2 + 1 - core}
    ways = ({"row": (z + 1) % n_row}, {"row": (z + n_row - 1) % n_row})

    barrier = pltpu.get_barrier_semaphore()
    for device in (*peers, pair, *ways):
        pl.semaphore_signal(barrier, inc=1, device_id=device, device_id_type=MESH)

    def load(i):
        part = pl.ds(pl.multiple_of(i * lines, lines), lines)
        return pltpu.make_async_copy(m_ref.at[part], o_ref.at[part], load_sem.at[i])

    for i in range(tiles):
        load(i).start()

    def widen(i):
        load(i).wait()
        part = pl.ds(pl.multiple_of(i * lines, lines), lines)
        wide[part] = o_ref[part].astype(F32)

    def piece(first, length, j, c):
        return pl.ds(first * 8 + 2 * c + j, length, stride=8)

    def tile(first, length, j):
        return jnp.concatenate([wide[piece(first, length, j, c), :] for c in range(4)], axis=1)

    def own_column(i):
        first = pl.multiple_of(i * NB, NB)
        panel[core, pl.ds(first, NB)] = tile(first, NB, 0).astype(BF16)

    widen(0)
    for source in range(2):
        @pl.when(z == source)
        def _():
            for j in range(2):
                rows[source, j] = tile(0, NB, j).astype(BF16)

    @pl.when(root)
    def _():
        own_column(0)

    depth = [pick(DEPTH[t], chip) for t in range(4)]
    owner = [pick(OWNER[d], chip) for d in range(4)]
    sender = []
    for d in range(4):
        value = depth[3]
        for t in range(3):
            value = jnp.where(owner[d] == t, depth[t], value)
        sender.append(value)

    away = (z - (1 - core) + n_row) % n_row
    farthest = jnp.where(away == 0, 0, jnp.maximum(away, n_row - away))
    late = jnp.maximum(zcount // 2 + ZLAG * farthest, plain)
    last_late = max(zcount // 2 + ZLAG * (n_row - 1), plain)

    pl.semaphore_wait(barrier, len(peers) + 3)

    def panel_step(k, hops):
        step = k - LAG * hops
        step_late = step - late + plain
        return jnp.where(step_late >= plain, step_late, jnp.where(step < plain, step, count))

    def panel_copy(t, s, device, send):
        ref = panel.at[core, pl.ds(pl.multiple_of((s * 4 + t) * CHUNK, CHUNK), CHUNK)]
        return pltpu.make_async_remote_copy(
            ref, ref, send, panel_recv.at[t * count + s], device_id=device, device_id_type=MESH
        )

    def slot(k, carry):
        for order in range(2):
            which = (order + 1 - core) % 2
            for way in range(2):
                hops = (z - which + n_row) % n_row
                if way:
                    hops = (n_row - hops) % n_row
                s = k - order * zcount - ZLAG * hops

                @pl.when((s >= 0) & (s < zcount))
                def _():
                    j = s // (zcount // 2)
                    first = way * (NB // 2) + s % (zcount // 2) * ZCHUNK
                    ref = rows.at[which, j, pl.ds(pl.multiple_of(first, ZCHUNK), ZCHUNK)]
                    copy = pltpu.make_async_remote_copy(
                        ref, ref, row_send.at[order * 2 + way], row_recv.at[(order * 2 + way) * zcount + s],
                        device_id=ways[way], device_id_type=MESH,
                    )

                    @pl.when(hops > 0)
                    def _():
                        copy.wait_recv()

                    @pl.when(hops < n_row - 1)
                    def _():
                        copy.start()

        @pl.when(root & (k == late))
        def _():
            panel[core, pl.ds(tiles * NB, NB)] = rows[1 - core, 0]

        for t in range(4):
            s = panel_step(k, depth[t])

            @pl.when((s >= 0) & (s < count) & jnp.logical_not(root))
            def _():
                panel_copy(t, s, pair, pair_send.at[0]).wait_recv()

        for d in range(4):
            s = panel_step(k, sender[d])

            @pl.when((s >= 0) & (s < count) & (owner[d] < 4))
            def _():
                panel_copy(owner[d], s, peers[d], panel_send.at[d]).start()

        for t in range(4):
            s = panel_step(k, depth[t])

            @pl.when((s >= 0) & (s < count))
            def _():
                ref = panel.at[core, pl.ds(pl.multiple_of((s * 4 + t) * CHUNK, CHUNK), CHUNK)]
                pltpu.make_async_remote_copy(
                    ref, ref, pair_send.at[0], pair_recv.at[(s * 4 + t) * CHUNK // NB],
                    device_id=pair, device_id_type=MESH,
                ).start()

        after = k // more + 1

        @pl.when((k % more == 0) & (after < tiles))
        def _():
            widen(after)

            @pl.when(root)
            def _():
                own_column(after)

        return carry

    slots = max(last_late + more + LAG * DEEPEST, 2 * zcount + ZLAG * (n_row - 1))
    lax.fori_loop(0, slots, slot, 0)

    def drain(ref, sem):
        pltpu.make_async_copy(ref, ref, sem).wait()

    for i in range(tiles + 1):
        drain(panel.at[1 - core, pl.ds(i * NB, NB)], pair_recv.at[i])
    for d in range(4):
        @pl.when(owner[d] < 4)
        def _():
            drain(panel.at[core, pl.ds(0, count * CHUNK)], panel_send.at[d])
    drain(panel.at[core], pair_send.at[0])
    for order in range(2):
        for way in range(2):
            hops = (z - (order + 1 - core) % 2 + n_row) % n_row
            if way:
                hops = (n_row - hops) % n_row

            @pl.when(hops < n_row - 1)
            def _():
                drain(rows.at[order, 0], row_send.at[order * 2 + way])

    end = pl.ds(tiles * NB, NB)
    extra[0] = dot(panel[0, end], upper_ref[0]).astype(BF16)
    extra[1] = dot(lower_ref[0], panel[1, end]).astype(BF16)
    for j in range(2):
        rows[0, j] = dot(lower_ref[0], rows[0, j]).astype(BF16)
        following = rows[1, j].astype(F32) - dot(extra[0], rows[0, j])
        rows[1, j] = dot(lower_ref[1], following.astype(BF16)).astype(BF16)

    def finish(i, carry):
        first = pl.multiple_of(i * NB, NB)
        here = pl.ds(first, NB)
        panel[0, here] = dot(panel[0, here], upper_ref[0]).astype(BF16)
        following = panel[1, here].astype(F32) - dot(panel[0, here], extra[1])
        panel[1, here] = dot(following.astype(BF16), upper_ref[1]).astype(BF16)
        g = i * n_row + z
        for j in range(2):
            h = j * n_col + col

            def update(k):
                def block(b, carry):
                    at = pl.multiple_of(first + b * 128, 128)
                    product = dot(panel[k, pl.ds(at, 128)], rows[k, j])
                    for c in range(4):
                        where = piece(at, 128, j, c)
                        wide[where, :] = wide[where, :] - product[:, c * 128 : (c + 1) * 128]
                    return carry

                lax.fori_loop(0, NB // 128, block, 0)

            def replace(value):
                for c in range(4):
                    wide[piece(first, NB, j, c), :] = value[:, c * 128 : (c + 1) * 128].astype(F32)

            for k in range(2):
                pl.when((g > k) & (h > k))(functools.partial(update, k))
                pl.when((g > k) & (h == k))(lambda k=k: replace(panel[k, here]))
                pl.when((g == k) & (h > k))(lambda k=k: replace(rows[k, j]))
        part = pl.ds(pl.multiple_of(i * lines, lines), lines)
        o_ref[part] = wide[part].astype(BF16)
        pltpu.make_async_copy(o_ref.at[part], out_ref.at[part], store_sem.at[i]).start()
        return carry

    lax.fori_loop(0, tiles, finish, 0)
    for i in range(tiles):
        part = pl.ds(i * lines, lines)
        pltpu.make_async_copy(o_ref.at[part], out_ref.at[part], store_sem.at[i]).wait()


def on_device(n_row, n_col, matrix, lower_inv, upper_inv):
    tiles = matrix.shape[0]
    lines = tiles * NB * 8
    count = (tiles + 1) * NB // (4 * CHUNK)
    split = matrix.reshape(tiles, NB, 2, 4, 128).transpose(0, 1, 3, 2, 4).reshape(lines, 128)
    out = pl.pallas_call(
        functools.partial(kernel, tiles, n_row, n_col),
        out_shape=jax.ShapeDtypeStruct((lines, 128), BF16),
        in_specs=[
            pl.BlockSpec(memory_space=pl.ANY),
            pl.BlockSpec(memory_space=pltpu.VMEM),
            pl.BlockSpec(memory_space=pltpu.VMEM),
        ],
        out_specs=pl.BlockSpec(memory_space=pl.ANY),
        scratch_shapes=[
            pltpu.VMEM((lines, 128), BF16),
            pltpu.VMEM((lines, 128), F32),
            pltpu.VMEM((2, (tiles + 1) * NB, NB), BF16),
            pltpu.VMEM((2, 2, NB, NB), BF16),
            pltpu.VMEM((2, NB, NB), BF16),
            pltpu.SemaphoreType.DMA((tiles,)),
            pltpu.SemaphoreType.DMA((tiles,)),
            pltpu.SemaphoreType.DMA((4 * count,)),
            pltpu.SemaphoreType.DMA((4,)),
            pltpu.SemaphoreType.DMA((tiles + 1,)),
            pltpu.SemaphoreType.DMA((1,)),
            pltpu.SemaphoreType.DMA((4 * (NB // ZCHUNK),)),
            pltpu.SemaphoreType.DMA((4,)),
        ],
        compiler_params=pltpu.CompilerParams(
            collective_id=1, has_side_effects=True, vmem_limit_bytes=48 << 20
        ),
    )(split, lower_inv, upper_inv)
    return out.reshape(tiles, NB, 4, 2, 128).transpose(0, 1, 3, 2, 4).reshape(matrix.shape)


def solution(mesh):
    placed = (P(None, "row", None, "col"), P(), P())
    return jax.shard_map(
        functools.partial(on_device, mesh.shape["row"], mesh.shape["col"]),
        mesh=mesh,
        in_specs=placed,
        out_specs=P(None, "row", None, "col"),
        check_vma=False,
    )
```

time: 461 us -> 111 us (0.24)
  waiting for transfers between devices: 383 us -> 0 us
  Pallas kernels: 0 us -> 101 us
  other arithmetic: 17.8 us -> 0 us
  matrix products: 17.7 us -> 0 us
  local copies, waits for them, and re-layouts: 24.2 us -> 9.19 us
  between operations: 13.3 us -> 0.01 us
    psum x4 -> x0, waiting for transfers between devices: 383 us -> none  [broadcast(): return lax.psum(block, axis)]
    pallas_call x0 -> x1, Pallas kernels: none -> 101 us  [on_device(): pl.pallas_call(functools.partial(kernel, tiles, n_row, n_col), out_shape=...]
    dot_general x2 -> x0, matrix products: 17.7 us -> none  [the longest x1 9.71 us: on_device(): jnp.dot(left_first, right_first, preferred_element_type=jnp.float32)]
    scatter x4 -> x0, other arithmetic: 11.3 us -> none  [the longest x2 7 us: write_column(): return schur.at[:, :tile_size].set(block)]
    reshape x1 -> x0, local copies, waits for them, and re-layouts: 11.1 us -> none  [on_device(): return schur.astype(jnp.bfloat16).reshape(matrix.shape)]
    select_n x4 -> x0, other arithmetic: 5.8 us -> none  [broadcast(): jnp.where(lax.axis_index(axis) == source, block, jnp.zeros_like(block))]
    unnamed x13 -> x5, local copies, waits for them, and re-layouts: 12.1 us -> 9.19 us
  transfers between devices with their start and end apart: 4 -> 0, of which waited for: 4 -> 0; matrix products, arithmetic and copies ran while one was open for 3% -> 0% of each run, Pallas kernels for 0% -> 0%
where the time goes in v1:
time: 111 us; the launch traced here: 110 us
  Pallas kernels  101 us (91%)
  local copies, waits for them, and re-layouts  9.19 us (8%)
    pallas_call x1, Pallas kernels, on_device(): pl.pallas_call(functools.partial(kernel, tiles, n_row, n_col), out_shape=...  101 us
    unnamed x5, local copies, waits for them, and re-layouts  9.19 us

profile of v1, /device:TPU:77, one launch (start us, length us, event | category | flops | bytes accessed | tf_op | source)
XLA Modules:
  0.0 110.4 jit_solution(3998968652551213793)
XLA Ops:
  0.0 0.0 copy-start
  0.0 1.2 %copy-done = bf16[2,512,512]{2,1,0:T(8,128)(2,1)S(1)} copy-done((bf16[2,512,512]{2,1,0:T(8,128)(2,1)S(1)}, bf16[2,512,512]{2,1,0:T(8,128)(2,1)}, u32[]{:S(2)}) %copy-start) | copy-done | bytes 1048600
  1.2 0.0 copy-start.1
  1.2 1.2 %copy-done.1 = bf16[2,512,512]{2,1,0:T(8,128)(2,1)S(1)} copy-done((bf16[2,512,512]{2,1,0:T(8,128)(2,1)S(1)}, bf16[2,512,512]{2,1,0:T(8,128)(2,1)}, u32[]{:S(2)}) %copy-start.1) | copy-done | bytes 1048600
  2.5 101.2 %shard_map.37 = bf16[24576,128]{1,0:T(8,128)(2,1)} custom-call(bf16[24576,128]{1,0:T(8,128)(2,1)} %bitcast.11, bf16[2,512,512]{2,1,0:T(8,128)(2,1)S(1)} %copy-done, bf16[2,512,512]{2,1,0:T(8,128)(2,1)S(1)} %copy-done.1), custom_call_target="tpu_custom_call" | custom-call | tf_op jit(solution)/shard_map/pallas_call | solution.py:289
  103.6 6.7 %copy.7 = bf16[6,512,2,512]{3,2,1,0:T(2,128)(2,1)} copy(bf16[6,512,2,512]{3,2,1,0:T(2,128)(2,1)} %bitcast.10) | data formatting | bytes 12582912
Async XLA Ops:
  0.0 1.2 %copy-start = (bf16[2,512,512]{2,1,0:T(8,128)(2,1)S(1)}, bf16[2,512,512]{2,1,0:T(8,128)(2,1)}, u32[]{:S(2)}) copy-start(bf16[2,512,512]{2,1,0:T(8,128)(2,1)} %lower_ref.1) | copy-start | bytes 3145732
  1.2 1.2 %copy-start.1 = (bf16[2,512,512]{2,1,0:T(8,128)(2,1)S(1)}, bf16[2,512,512]{2,1,0:T(8,128)(2,1)}, u32[]{:S(2)}) copy-start(bf16[2,512,512]{2,1,0:T(8,128)(2,1)} %upper_ref.1) | copy-start | bytes 3145732

commit v2 on v1

--- a/solution.py
+++ b/solution.py
@@ -17,8 +17,8 @@
     (1, 2): 1, (2, 2): 0, (3, 2): 0, (0, 3): 2, (1, 3): 3, (2, 3): 3, (3, 3): 0,
 }
 CHUNK = 64
-ZCHUNK = 32
-LAG, ZLAG = 5, 5
+ZCHUNK = 64
+LAG, ZLAG = 4, 3
 
 
 def trees():
@@ -59,8 +59,8 @@
 
 
 def kernel(
-    tiles, n_row, n_col, m_ref, lower_ref, upper_ref, out_ref, o_ref, wide, panel, rows, extra,
-    load_sem, store_sem, panel_recv, panel_send, pair_recv, pair_send, row_recv, row_send,
+    tiles, n_row, n_col, m_ref, lower_hbm, upper_hbm, out_ref, o_ref, wide, total, panel, low, rows, high, extra,
+    lower_ref, upper_ref, load_sem, weight_sem, store_sem, panel_recv, panel_send, pair_recv, pair_send, row_recv, row_send,
 ):
     z, col = lax.axis_index("row"), lax.axis_index("col")
     core, chip = col % 2, col // 2
@@ -86,30 +86,36 @@
         part = pl.ds(pl.multiple_of(i * lines, lines), lines)
         return pltpu.make_async_copy(m_ref.at[part], o_ref.at[part], load_sem.at[i])
 
+    weights = (
+        pltpu.make_async_copy(lower_hbm, lower_ref, weight_sem.at[0]),
+        pltpu.make_async_copy(upper_hbm, upper_ref, weight_sem.at[1]),
+    )
     for i in range(tiles):
         load(i).start()
+    for copy in weights:
+        copy.start()
+
+    def piece(first, length, j, c):
+        return pl.ds(first * 8 + 2 * c + j, length, stride=8)
 
     def widen(i):
         load(i).wait()
-        part = pl.ds(pl.multiple_of(i * lines, lines), lines)
-        wide[part] = o_ref[part].astype(F32)
-
-    def piece(first, length, j, c):
-        return pl.ds(first * 8 + 2 * c + j, length, stride=8)
-
-    def tile(first, length, j):
-        return jnp.concatenate([wide[piece(first, length, j, c), :] for c in range(4)], axis=1)
+        wide[...] = o_ref[pl.ds(pl.multiple_of(i * lines, lines), lines)].astype(F32)
+        for j in range(2):
+            for c in range(4):
+                part = wide[piece(0, NB, j, c), :]
+                total[j, pl.ds(pl.multiple_of(i * NB, NB), NB), c * 128 : (c + 1) * 128] = part
 
     def own_column(i):
-        first = pl.multiple_of(i * NB, NB)
-        panel[core, pl.ds(first, NB)] = tile(first, NB, 0).astype(BF16)
+        here = pl.ds(pl.multiple_of(i * NB, NB), NB)
+        panel[core, here] = total[0, here].astype(BF16)
 
     widen(0)
     for source in range(2):
         @pl.when(z == source)
         def _():
             for j in range(2):
-                rows[source, j] = tile(0, NB, j).astype(BF16)
+                rows[source, j] = total[j, pl.ds(0, NB)].astype(BF16)
 
     @pl.when(root)
     def _():
@@ -208,16 +214,48 @@
             def _():
                 own_column(after)
 
+        i = (k - first_low) // 2
+
+        @pl.when((k >= first_low) & ((k - first_low) % 2 == 0) & (i < tiles))
+        def _():
+            here = pl.ds(pl.multiple_of(i * NB, NB), NB)
+
+            @pl.when(core == 1)
+            def _():
+                drain(panel.at[0, here], pair_recv.at[i])
+
+            low[here] = dot(panel[0, here], upper_ref[0]).astype(BF16)
+
+        @pl.when((k >= rows_in) & (k < rows_in + 2))
+        def _():
+            high[k - rows_in] = dot(lower_ref[0], rows[0, k - rows_in]).astype(BF16)
+
+        for b in range(3):
+            unit = (k - rows_in - 2) * 3 + b
+            i, j = unit // 4, unit // 2 % 2
+
+            @pl.when((unit >= 0) & (unit < 4 * tiles) & (i * n_row + z > 0) & (j * n_col + col > 0))
+            def _():
+                half = pl.ds(pl.multiple_of(i * NB + unit % 2 * (NB // 2), NB // 2), NB // 2)
+                total[j, half] = total[j, half] - dot(low[half], high[j])
+
         return carry
-
-    slots = max(last_late + more + LAG * DEEPEST, 2 * zcount + ZLAG * (n_row - 1))
-    lax.fori_loop(0, slots, slot, 0)
 
     def drain(ref, sem):
         pltpu.make_async_copy(ref, ref, sem).wait()
 
-    for i in range(tiles + 1):
-        drain(panel.at[1 - core, pl.ds(i * NB, NB)], pair_recv.at[i])
+    for copy in weights:
+        copy.wait()
+    first_low = more - 1 + LAG * DEEPEST + 1
+    rows_in = max(2 * zcount + ZLAG * (n_row - 1), first_low + 2 * tiles)
+    slots = max(last_late + more + LAG * DEEPEST, rows_in + 2 + (4 * tiles + 2) // 3)
+    lax.fori_loop(0, slots, slot, 0)
+
+    for i in range(tiles):
+        @pl.when(core == 0)
+        def _():
+            drain(panel.at[1, pl.ds(i * NB, NB)], pair_recv.at[i])
+    drain(panel.at[1 - core, pl.ds(tiles * NB, NB)], pair_recv.at[tiles])
     for d in range(4):
         @pl.when(owner[d] < 4)
         def _():
@@ -237,41 +275,52 @@
     extra[0] = dot(panel[0, end], upper_ref[0]).astype(BF16)
     extra[1] = dot(lower_ref[0], panel[1, end]).astype(BF16)
     for j in range(2):
-        rows[0, j] = dot(lower_ref[0], rows[0, j]).astype(BF16)
-        following = rows[1, j].astype(F32) - dot(extra[0], rows[0, j])
+        following = rows[1, j].astype(F32) - dot(extra[0], high[j])
         rows[1, j] = dot(lower_ref[1], following.astype(BF16)).astype(BF16)
 
     def finish(i, carry):
         first = pl.multiple_of(i * NB, NB)
         here = pl.ds(first, NB)
-        panel[0, here] = dot(panel[0, here], upper_ref[0]).astype(BF16)
-        following = panel[1, here].astype(F32) - dot(panel[0, here], extra[1])
+        following = panel[1, here].astype(F32) - dot(low[here], extra[1])
         panel[1, here] = dot(following.astype(BF16), upper_ref[1]).astype(BF16)
         g = i * n_row + z
+
+        def spread(j, start, value):
+            for c in range(4):
+                wide[piece(start, value.shape[0], j, c), :] = value[:, c * 128 : (c + 1) * 128]
+
         for j in range(2):
             h = j * n_col + col
-
-            def update(k):
-                def block(b, carry):
-                    at = pl.multiple_of(first + b * 128, 128)
-                    product = dot(panel[k, pl.ds(at, 128)], rows[k, j])
-                    for c in range(4):
-                        where = piece(at, 128, j, c)
-                        wide[where, :] = wide[where, :] - product[:, c * 128 : (c + 1) * 128]
-                    return carry
-
-                lax.fori_loop(0, NB // 128, block, 0)
-
-            def replace(value):
-                for c in range(4):
-                    wide[piece(first, NB, j, c), :] = value[:, c * 128 : (c + 1) * 128].astype(F32)
-
-            for k in range(2):
-                pl.when((g > k) & (h > k))(functools.partial(update, k))
-                pl.when((g > k) & (h == k))(lambda k=k: replace(panel[k, here]))
-                pl.when((g == k) & (h > k))(lambda k=k: replace(rows[k, j]))
+            both = (g > 1) & (h > 1)
+
+            @pl.when(both)
+            def _():
+                for b in range(4):
+                    at = pl.ds(pl.multiple_of(first + b * 128, 128), 128)
+                    spread(j, b * 128, total[j, at] - dot(panel[1, at], rows[1, j]))
+
+            @pl.when(jnp.logical_not(both))
+            def _():
+                @pl.when((g > 0) & (h == 0))
+                def _():
+                    total[j, here] = low[here].astype(F32)
+
+                @pl.when((g > 1) & (h == 1))
+                def _():
+                    total[j, here] = panel[1, here].astype(F32)
+
+                @pl.when((g == 0) & (h > 0))
+                def _():
+                    total[j, here] = high[j].astype(F32)
+
+                @pl.when((g == 1) & (h > 1))
+                def _():
+                    total[j, here] = rows[1, j].astype(F32)
+
+                spread(j, 0, total[j, here])
+
         part = pl.ds(pl.multiple_of(i * lines, lines), lines)
-        o_ref[part] = wide[part].astype(BF16)
+        o_ref[part] = wide[...].astype(BF16)
         pltpu.make_async_copy(o_ref.at[part], out_ref.at[part], store_sem.at[i]).start()
         return carry
 
@@ -279,6 +328,10 @@
     for i in range(tiles):
         part = pl.ds(i * lines, lines)
         pltpu.make_async_copy(o_ref.at[part], out_ref.at[part], store_sem.at[i]).wait()
+
+
+def hand_on(x_ref, o_ref):
+    o_ref[...] = x_ref[...]
 
 
 def on_device(n_row, n_col, matrix, lower_inv, upper_inv):
@@ -290,18 +343,24 @@
         functools.partial(kernel, tiles, n_row, n_col),
         out_shape=jax.ShapeDtypeStruct((lines, 128), BF16),
         in_specs=[
-            pl.BlockSpec(memory_space=pl.ANY),
-            pl.BlockSpec(memory_space=pltpu.VMEM),
-            pl.BlockSpec(memory_space=pltpu.VMEM),
+            pl.BlockSpec(memory_space=pltpu.HBM),
+            pl.BlockSpec(memory_space=pltpu.HBM),
+            pl.BlockSpec(memory_space=pltpu.HBM),
         ],
         out_specs=pl.BlockSpec(memory_space=pl.ANY),
         scratch_shapes=[
             pltpu.VMEM((lines, 128), BF16),
-            pltpu.VMEM((lines, 128), F32),
+            pltpu.VMEM((8 * NB, 128), F32),
+            pltpu.VMEM((2, tiles * NB, NB), F32),
             pltpu.VMEM((2, (tiles + 1) * NB, NB), BF16),
+            pltpu.VMEM((tiles * NB, NB), BF16),
             pltpu.VMEM((2, 2, NB, NB), BF16),
             pltpu.VMEM((2, NB, NB), BF16),
+            pltpu.VMEM((2, NB, NB), BF16),
+            pltpu.VMEM((2, NB, NB), BF16),
+            pltpu.VMEM((2, NB, NB), BF16),
             pltpu.SemaphoreType.DMA((tiles,)),
+            pltpu.SemaphoreType.DMA((2,)),
             pltpu.SemaphoreType.DMA((tiles,)),
             pltpu.SemaphoreType.DMA((4 * count,)),
             pltpu.SemaphoreType.DMA((4,)),
@@ -314,6 +373,15 @@
             collective_id=1, has_side_effects=True, vmem_limit_bytes=48 << 20
         ),
     )(split, lower_inv, upper_inv)
+    block = pl.BlockSpec((NB * 16, 128), lambda i: (i, 0))
+    out = pl.pallas_call(
+        hand_on,
+        out_shape=jax.ShapeDtypeStruct((lines, 128), BF16),
+        grid=(lines // (NB * 16),),
+        in_specs=[block],
+        out_specs=block,
+        compiler_params=pltpu.CompilerParams(vmem_limit_bytes=32 << 20),
+    )(out)
     return out.reshape(tiles, NB, 4, 2, 128).transpose(0, 1, 3, 2, 4).reshape(matrix.shape)
 
 

time: 111 us -> 88.6 us (0.80)
  the two profiles are of different devices: /device:TPU:77 before, /device:TPU:70 now
where the time goes in v2:
time: 88.6 us; the launch traced here: 88.4 us
  Pallas kernels  83.2 us (94%)
  local copies, waits for them, and re-layouts  5.23 us (6%)
    pallas_call x1, Pallas kernels, on_device(): pl.pallas_call(functools.partial(kernel, tiles, n_row, n_col), out_shape=...  80.2 us
    unnamed x6, local copies, waits for them, and re-layouts  5.23 us
    pallas_call x1, Pallas kernels, on_device(): pl.pallas_call(hand_on, out_shape=jax.ShapeDtypeStruct((lines, 128), BF16...  2.91 us

profile of v2, /device:TPU:70, one launch (start us, length us, event | category | flops | bytes accessed | tf_op | source)
XLA Modules:
  0.0 88.4 jit_solution(13399509880449188004)
XLA Ops:
  0.0 0.0 copy-start.1
  0.0 1.2 %copy-done.1 = bf16[2,512,512]{2,1,0:T(8,128)(2,1)S(1)} copy-done((bf16[2,512,512]{2,1,0:T(8,128)(2,1)S(1)}, bf16[2,512,512]{2,1,0:T(8,128)(2,1)}, u32[]{:S(2)}) %copy-start.1) | copy-done | bytes 1048600
  1.2 0.0 copy-start.2
  1.2 1.2 %copy-done.2 = bf16[2,512,512]{2,1,0:T(8,128)(2,1)S(1)} copy-done((bf16[2,512,512]{2,1,0:T(8,128)(2,1)S(1)}, bf16[2,512,512]{2,1,0:T(8,128)(2,1)}, u32[]{:S(2)}) %copy-start.2) | copy-done | bytes 1048600
  2.5 80.2 %shard_map.37.x_ref = bf16[24576,128]{1,0:T(8,128)(2,1)} custom-call(bf16[24576,128]{1,0:T(8,128)(2,1)} %bitcast.10, bf16[2,512,512]{2,1,0:T(8,128)(2,1)S(1)} %copy-done.1, bf16[2,512,512]{2,1,0:T(8,128)(2,1)S(1)} %copy-done.2), custom_call_target="tpu_custom_call" | custom-call | tf_op jit(solution)/shard_map/pallas_call | solution.py:342
  82.7 0.0 copy-start
  82.7 2.8 %copy-done = bf16[24576,128]{1,0:T(8,128)(2,1)S(1)} copy-done((bf16[24576,128]{1,0:T(8,128)(2,1)S(1)}, bf16[24576,128]{1,0:T(8,128)(2,1)}, u32[]{:S(2)}) %copy-start) | copy-done | bytes 6291480
  85.5 2.9 %shard_map.38 = bf16[24576,128]{1,0:T(8,128)(2,1)} custom-call(bf16[24576,128]{1,0:T(8,128)(2,1)S(1)} %copy-done), custom_call_target="tpu_custom_call" | custom-call | tf_op jit(solution)/shard_map/pallas_call | solution.py:377
Async XLA Ops:
  0.0 1.2 %copy-start.1 = (bf16[2,512,512]{2,1,0:T(8,128)(2,1)S(1)}, bf16[2,512,512]{2,1,0:T(8,128)(2,1)}, u32[]{:S(2)}) copy-start(bf16[2,512,512]{2,1,0:T(8,128)(2,1)} %lower_hbm.1) | copy-start | bytes 3145732
  1.2 1.2 %copy-start.2 = (bf16[2,512,512]{2,1,0:T(8,128)(2,1)S(1)}, bf16[2,512,512]{2,1,0:T(8,128)(2,1)}, u32[]{:S(2)}) copy-start(bf16[2,512,512]{2,1,0:T(8,128)(2,1)} %upper_hbm.1) | copy-start | bytes 3145732
  82.7 2.8 %copy-start = (bf16[24576,128]{1,0:T(8,128)(2,1)S(1)}, bf16[24576,128]{1,0:T(8,128)(2,1)}, u32[]{:S(2)}) copy-start(bf16[24576,128]{1,0:T(8,128)(2,1)} %shard_map.37.x_ref) | copy-start | bytes 18874372

commit v3 on v2

--- a/solution.py
+++ b/solution.py
@@ -281,23 +281,38 @@
     def finish(i, carry):
         first = pl.multiple_of(i * NB, NB)
         here = pl.ds(first, NB)
-        following = panel[1, here].astype(F32) - dot(low[here], extra[1])
-        panel[1, here] = dot(following.astype(BF16), upper_ref[1]).astype(BF16)
         g = i * n_row + z
+        inner = (g > 1) & (col > 1)
 
         def spread(j, start, value):
             for c in range(4):
                 wide[piece(start, value.shape[0], j, c), :] = value[:, c * 128 : (c + 1) * 128]
 
+        def solve(at):
+            following = panel[1, at].astype(F32) - dot(low[at], extra[1])
+            return dot(following.astype(BF16), upper_ref[1]).astype(BF16)
+
+        @pl.when(inner)
+        def _():
+            for b in range(2):
+                at = pl.ds(pl.multiple_of(first + b * 256, 256), 256)
+                lower = solve(at)
+                for j in range(2):
+                    spread(j, b * 256, total[j, at] - dot(lower, rows[1, j]))
+
+        @pl.when(jnp.logical_not(inner))
+        def _():
+            panel[1, here] = solve(here)
+
         for j in range(2):
             h = j * n_col + col
             both = (g > 1) & (h > 1)
 
-            @pl.when(both)
-            def _():
-                for b in range(4):
-                    at = pl.ds(pl.multiple_of(first + b * 128, 128), 128)
-                    spread(j, b * 128, total[j, at] - dot(panel[1, at], rows[1, j]))
+            @pl.when(both & jnp.logical_not(inner))
+            def _():
+                for b in range(2):
+                    at = pl.ds(pl.multiple_of(first + b * 256, 256), 256)
+                    spread(j, b * 256, total[j, at] - dot(panel[1, at], rows[1, j]))
 
             @pl.when(jnp.logical_not(both))
             def _():
@@ -370,7 +385,7 @@
             pltpu.SemaphoreType.DMA((4,)),
         ],
         compiler_params=pltpu.CompilerParams(
-            collective_id=1, has_side_effects=True, vmem_limit_bytes=48 << 20
+            collective_id=1, has_side_effects=True, vmem_limit_bytes=60 << 20
         ),
     )(split, lower_inv, upper_inv)
     block = pl.BlockSpec((NB * 16, 128), lambda i: (i, 0))

time: 88.6 us -> 86.9 us (0.981)
  the two profiles are of different devices: /device:TPU:70 before, /device:TPU:77 now
where the time goes in v3:
time: 86.9 us; the launch traced here: 85.2 us
  Pallas kernels  82.4 us (95%)
  local copies, waits for them, and re-layouts  2.78 us (3%)
    pallas_call x1, Pallas kernels, on_device(): pl.pallas_call(functools.partial(kernel, tiles, n_row, n_col), out_shape=...  79.5 us
    pallas_call x1, Pallas kernels, on_device(): pl.pallas_call(hand_on, out_shape=jax.ShapeDtypeStruct((lines, 128), BF16...  2.91 us
    unnamed x2, local copies, waits for them, and re-layouts  2.78 us

profile of v3, /device:TPU:77, one launch (start us, length us, event | category | flops | bytes accessed | tf_op | source)
XLA Modules:
  0.0 85.2 jit_solution(16383176894788107124)
XLA Ops:
  0.0 79.5 %shard_map.37.x_ref = bf16[24576,128]{1,0:T(8,128)(2,1)} custom-call(bf16[24576,128]{1,0:T(8,128)(2,1)} %bitcast.10, bf16[2,512,512]{2,1,0:T(8,128)(2,1)} %lower_hbm.1, bf16[2,512,512]{2,1,0:T(8,128)(2,1)} %upper_hbm.1), custom_call_target="tpu_custom_call" | custom-call | tf_op jit(solution)/shard_map/pallas_call | solution.py:357
  79.5 0.0 copy-start
  79.5 2.8 %copy-done = bf16[24576,128]{1,0:T(8,128)(2,1)S(1)} copy-done((bf16[24576,128]{1,0:T(8,128)(2,1)S(1)}, bf16[24576,128]{1,0:T(8,128)(2,1)}, u32[]{:S(2)}) %copy-start) | copy-done | bytes 6291480
  82.3 2.9 %shard_map.38 = bf16[24576,128]{1,0:T(8,128)(2,1)} custom-call(bf16[24576,128]{1,0:T(8,128)(2,1)S(1)} %copy-done), custom_call_target="tpu_custom_call" | custom-call | tf_op jit(solution)/shard_map/pallas_call | solution.py:392
Async XLA Ops:
  79.5 2.8 %copy-start = (bf16[24576,128]{1,0:T(8,128)(2,1)S(1)}, bf16[24576,128]{1,0:T(8,128)(2,1)}, u32[]{:S(2)}) copy-start(bf16[24576,128]{1,0:T(8,128)(2,1)} %shard_map.37.x_ref) | copy-start | bytes 18874372
